TPU v7x, 32 devices: a whole 2x2x4 slice. The times are simulated.
32 devices in a mesh: batch: 4 (over y, x), ctx: 8 (over z, core).
Axes of the slice: x: 2, y: 2, z: 4, core: 2. Of those that a mesh axis runs over, the one named last changes fastest.
Arguments:
- inner_x: bfloat16 [4, 512, 8192], P('batch', 'ctx'), may hold values from -6 to 6
- inner_bc: bfloat16 [4, 512, 1024], P('batch', 'ctx'), may hold values from -6 to 6
- step_size: float32 [4, 512, 64], P('batch', 'ctx'), may hold values from 0.1 to 1400, as said below
- decay_base: float32 [64], replicated, may hold values from 0.9995 to 0.9998
- conv_inner: float32 [4, 8192], replicated, may hold values from -3 to 3
- conv_groups: float32 [4, 1024], replicated, may hold values from -3 to 3
- norm_gain: float32 [8192], replicated, may hold values from 0.5 to 1.5
- cache_pool: bfloat16 [16, 64, 128, 128], P('batch', 'ctx'), may hold values from -0.59765625 to 0.59765625
- reuse_owner: int32 [4], replicated, may hold values from 0 to 3
- reuse_level: int32 [4], replicated, may hold values from 0 to 4, as said below
- prompt_blocks: int32 [4], replicated, may hold values from 1 to 2
Outputs:
- mixer_out: bfloat16 [4, 512, 8192], P('batch', 'ctx')
Inputs may be any that keep to these rules, and one draw needn't show every extreme that they name: `step_size`: positive step sizes. `reuse_level`: 0 means nothing is cached; level l names the owner's l-th cached state.
All inputs are finite; a program needn't handle non-finite values.
Results may differ from a plain program's by a relative error of at most 0.009.
Values may be sent and summed in bfloat16 or wider, within the bound.
A program may use at most 64 MiB of HBM per device.

v0:
```python
import jax
import jax.numpy as jnp
from jax import lax
from jax.sharding import PartitionSpec as P

LOCAL_HEADS = 64
P_SIZE = 128
N = 128
GROUPS = 4
KCONV = 4
LEN_BLOCK = 256


def shifted(value, axis, steps):
    count = lax.axis_size(axis)
    first, last = (max(0, -steps), min(count, count - steps))
    return lax.ppermute(value, axis, [(source, source + steps) for source in range(first, last)])


def convolve(extended, weight, length):
    summed = jnp.zeros((length, extended.shape[1]), jnp.float32)
    for offset in range(weight.shape[0]):
        summed = summed + weight[offset] * extended[offset : offset + length].astype(jnp.float32)
    return jax.nn.silu(summed).astype(jnp.bfloat16)


def block_local(conv_x, write_proj, read_proj, log_step):
    length = log_step.shape[0]
    per_group = LOCAL_HEADS // GROUPS
    cumul = jnp.cumsum(log_step, axis=0)
    inject = -jnp.expm1(log_step)
    inner_heads = conv_x.reshape(length, GROUPS, per_group, P_SIZE)
    write_groups = write_proj.reshape(length, GROUPS, N)
    read_groups = read_proj.reshape(length, GROUPS, N)
    scores = jnp.einsum(
        "tgn,sgn->gts", read_groups, write_groups, preferred_element_type=jnp.float32
    )
    row_index = jnp.arange(length)[:, None]
    col_index = jnp.arange(length)[None, :]
    cumul_heads = cumul.T.reshape(GROUPS, per_group, length)
    inject_heads = inject.T.reshape(GROUPS, per_group, length)
    exponent_gap = cumul_heads[:, :, :, None] - cumul_heads[:, :, None, :]
    exponent_gap = jnp.where(row_index >= col_index, exponent_gap, -jnp.inf)
    mixing = (scores[:, None] * jnp.exp(exponent_gap) * inject_heads[:, :, None, :]).astype(
        jnp.bfloat16
    )
    intra_part = jnp.einsum(
        "gkts,sgkp->tgkp", mixing, inner_heads, preferred_element_type=jnp.float32
    )
    tail_weight = jnp.exp(cumul[-1][None, :] - cumul) * inject
    weighted = (inner_heads * tail_weight.reshape(length, GROUPS, per_group)[..., None]).astype(
        jnp.bfloat16
    )
    end_state = jnp.einsum(
        "sgkp,sgn->gkpn", weighted, write_groups, preferred_element_type=jnp.float32
    )
    end_state = end_state.reshape(LOCAL_HEADS, P_SIZE, N).astype(jnp.bfloat16)
    block_decay = jnp.exp(cumul[-1]).astype(jnp.bfloat16)
    return (intra_part.reshape(length, LOCAL_HEADS, P_SIZE), cumul, end_state, block_decay)


def block_output(intra_part, cumul, read_proj, incoming, norm_gain, live):
    length = cumul.shape[0]
    per_group = LOCAL_HEADS // GROUPS
    read_groups = read_proj.reshape(length, GROUPS, N)
    state_groups = incoming.reshape(GROUPS, per_group, P_SIZE, N)
    inter_part = jnp.einsum(
        "tgn,gkpn->tgkp", read_groups, state_groups, preferred_element_type=jnp.float32
    ).reshape(length, LOCAL_HEADS, P_SIZE)
    summed = intra_part + jnp.exp(cumul)[:, :, None] * inter_part
    inv_scale = lax.rsqrt(jnp.mean(summed * summed, axis=2, keepdims=True) + 1e-05)
    result = summed * inv_scale * norm_gain.reshape(LOCAL_HEADS, P_SIZE)
    result = jnp.where(live[:, None, None], result, 0.0)
    return result.reshape(length, LOCAL_HEADS * P_SIZE).astype(jnp.bfloat16)


def advance(running, pieces):
    decay_block, state_block = pieces
    next_state = decay_block.astype(jnp.float32)[:, None, None] * running + state_block.astype(
        jnp.float32
    )
    return (next_state, running)


def body(
    inner_x,
    inner_bc,
    step_size,
    decay_base,
    conv_inner,
    conv_groups,
    norm_gain,
    cache_pool,
    reuse_owner,
    reuse_level,
    prompt_blocks,
):
    length = inner_x.shape[1]
    width_x = inner_x.shape[2]
    request = lax.axis_index("batch")
    ctx_place = lax.axis_index("ctx")
    tail_rows = jnp.concatenate(
        [inner_x[0, length - KCONV + 1 :], inner_bc[0, length - KCONV + 1 :]], axis=1
    )
    tail_rows = shifted(tail_rows, "ctx", 1)
    conv_x = convolve(
        jnp.concatenate([tail_rows[:, :width_x], inner_x[0]], axis=0), conv_inner, length
    )
    conv_bc = convolve(
        jnp.concatenate([tail_rows[:, width_x:], inner_bc[0]], axis=0), conv_groups, length
    )
    positions = ctx_place * length + jnp.arange(length)
    live = positions < prompt_blocks[request] * LEN_BLOCK
    log_step = jnp.where(live[:, None], step_size[0], 0.0) * jnp.log(decay_base)[None, :]
    intra_part, cumul, end_state, block_decay = block_local(
        conv_x, conv_bc[:, : GROUPS * N], conv_bc[:, GROUPS * N :], log_step
    )
    cache_owner = reuse_owner[request]
    cached_level = reuse_level[request]
    slots = cache_pool.shape[0]
    pooled = lax.all_gather(cache_pool, "batch", axis=0, tiled=True)
    slot_index = cache_owner * slots + jnp.maximum(cached_level - 1, 0)
    start_state = lax.dynamic_index_in_dim(pooled, slot_index, 0, keepdims=False)
    start_state = jnp.where(cached_level > 0, start_state, jnp.zeros_like(start_state))
    ctx_count = lax.axis_size("ctx")
    head_share = LOCAL_HEADS // ctx_count
    decays_in, states_in = (
        lax.all_to_all(
            block_decay.reshape(ctx_count, head_share),
            "ctx",
            split_axis=0,
            concat_axis=0,
            tiled=True,
        ),
        lax.all_to_all(
            end_state.reshape(ctx_count, head_share, P_SIZE, N),
            "ctx",
            split_axis=0,
            concat_axis=0,
            tiled=True,
        ),
    )
    last_state, incoming_parts = lax.scan(
        advance, start_state.astype(jnp.float32), (decays_in, states_in)
    )
    returned = lax.all_to_all(
        incoming_parts.astype(jnp.bfloat16), "ctx", split_axis=0, concat_axis=0, tiled=True
    )
    incoming = returned.reshape(LOCAL_HEADS, P_SIZE, N)
    result = block_output(intra_part, cumul, conv_bc[:, GROUPS * N :], incoming, norm_gain, live)
    return result.reshape(1, length, LOCAL_HEADS * P_SIZE)


def solution(mesh):
    return jax.shard_map(
        body,
        mesh=mesh,
        in_specs=(
            P("batch", "ctx", None),
            P("batch", "ctx", None),
            P("batch", "ctx", None),
            P(),
            P(),
            P(),
            P(),
            P("batch", "ctx", None, None),
            P(),
            P(),
            P(),
        ),
        out_specs=P("batch", "ctx", None),
        check_vma=False,
    )
```

profile of v0, /device:TPU:0, one launch (start us, length us, event | category | flops | bytes accessed | tf_op | source)
XLA Modules:
  0.0 178.9 jit_solution(856277272822642632)
XLA Ops:
  6.5 0.7 all-gather.2.cloned.1.call-update
  7.3 0.9 slice_bitcast_fusion
  8.2 0.7 slice_bitcast_fusion.1
  9.0 2.4 %collective-permute-start = (bf16[3,9216]{1,0:T(4,128)(2,1)S(1)}, bf16[3,9216]{1,0:T(4,128)(2,1)S(1)}, u32[]{:S(2)}, u32[]{:S(2)}) collective-permute-start(bf16[3,9216]{1,0:T(4,128)(2,1)S(1)} %pad_maximum_fusion.2), channel_id=1, source_target_pairs={{0,1},{1,2},{2,3},{3,4},{4,5},{5,6},{6,7},{8,9},{9,10},{10,11},{11... | collective-permute-start | bytes 165896 | tf_op jit(solution)/shard_map/ppermute | solution.py:17
  11.3 0.8 copy.48
  12.2 0.7 log.3
  12.8 1.2 dynamic_slice.21
  15.1 0.7 convert_element_type.119
  15.8 6.2 %all-to-all-start = ((bf16[8,1,8]{2,1,0:T(2,128)(2,1)}), bf16[8,1,8]{2,1,0:T(2,128)(2,1)S(1)}, u32[]{:S(2)}, u32[]{:S(2)}) async-start(bf16[8,1,8]{2,1,0:T(2,128)(2,1)} %convert_element_type.119), calls=%async_computation | async-start | bytes 8192 | tf_op jit(solution)/shard_map/all_to_all | solution.py:128
  22.3 1.3 fusion.32
  23.6 0.2 multiply_convert_fusion.5
  23.9 1.6 fusion.16
  25.5 0.3 copy.70
  25.8 1.0 copy-done
  26.8 3.4 %convolution_convert_fusion = bf16[4,16,128,128]{3,2,1,0:T(8,128)(2,1)} fusion(f32[64,4,16]{0,2,1:T(8,128)S(1)} %get-tuple-element.54, bf16[64,4,16,128]{3,2,1,0:T(8,128)(2,1)S(1)} %bitcast.84, bf16[64,4,128,1]{2,1,0,3:T(4,128)(2,1)S(1)} %bitcast.90), kind=kOutput, calls=%fused_computation.12 | convolution fusion | flops 136839168 | bytes 3227648 | tf_op jit(solution)/shard_map/sgkp,sgn->gkpn/dot_general | solution.py:54
  30.2 5.2 %all-to-all-start.1 = ((bf16[8,8,128,128]{3,2,1,0:T(8,128)(2,1)}), bf16[8,8,128,128]{3,2,1,0:T(8,128)(2,1)S(1)}, u32[]{:S(2)}, u32[]{:S(2)}) async-start(bf16[8,8,128,128]{3,2,1,0:T(8,128)(2,1)} %bitcast.28), calls=%async_computation.1 | async-start | bytes 4194304 | tf_op jit(solution)/shard_map/all_to_all | solution.py:135
  35.4 0.6 dynamic_slice.22
  37.3 0.6 dynamic_slice.23
  38.6 26.1 %all-gather.2.cloned.1.call-done = bf16[16,8,128,128]{3,2,1,0:T(8,128)(2,1)} async-done(((bf16[4,8,128,128]{3,2,1,0:T(8,128)(2,1)}), bf16[16,8,128,128]{3,2,1,0:T(8,128)(2,1)}) %all-gather.2.cloned.1.call-update) | async-done | bytes 4194320 | tf_op jit(solution)/shard_map/all_gather | solution.py:121
  64.6 1.0 bitcast_convert_fusion
  65.6 18.9 %all-to-all-done.1 = bf16[8,8,128,128]{3,2,1,0:T(8,128)(2,1)S(1)} async-done(((bf16[8,8,128,128]{3,2,1,0:T(8,128)(2,1)}), bf16[8,8,128,128]{3,2,1,0:T(8,128)(2,1)S(1)}, u32[]{:S(2)}, u32[]{:S(2)}) %all-to-all-start.1) | async-done | bytes 2097184 | tf_op jit(solution)/shard_map/all_to_all | solution.py:135
  84.5 7.4 %while.12 = (s32[]{:T(128)}, f32[8,128,128]{2,1,0:T(8,128)S(1)}, bf16[8,8,128,128]{3,2,1,0:T(8,128)(2,1)}, bf16[8,8]{1,0:T(8,128)(2,1)S(1)}, bf16[8,8,128,128]{3,2,1,0:T(8,128)(2,1)S(1)}, /*index=5*/s32[]{:T(128)}) while((s32[]{:T(128)}, f32[8,128,128]{2,1,0:T(8,128)S(1)}, bf16[8,8,128,128]{3,2,1,0:T(8,128)(2,1)}, bf16[8,8]{1,0:T(8,128)(2,1)S(1)}, ...), condition=%wide.region_2.3_spmd, body=%wide.region_1.2_spmd.sunk | while | flops 393226 | bytes 2359965 | solution.py:143
  84.5 0.7 bitcast_dynamic-update-slice_fusion.2
  85.2 0.2 convert_add_fusion.2
  85.4 0.7 bitcast_dynamic-update-slice_fusion.2
  86.2 0.2 convert_add_fusion.2
  86.3 0.8 bitcast_dynamic-update-slice_fusion.2
  87.1 0.2 convert_add_fusion.2
  87.3 0.7 bitcast_dynamic-update-slice_fusion.2
  88.0 0.2 convert_add_fusion.2
  88.2 0.8 bitcast_dynamic-update-slice_fusion.2
  89.0 0.2 convert_add_fusion.2
  89.1 0.8 bitcast_dynamic-update-slice_fusion.2
  90.1 0.8 bitcast_dynamic-update-slice_fusion.2
  91.0 0.7 bitcast_dynamic-update-slice_fusion.2
  91.9 4.4 %all-to-all-start.2 = ((bf16[8,8,128,128]{3,2,1,0:T(8,128)(2,1)}), bf16[8,8,128,128]{3,2,1,0:T(8,128)(2,1)}, u32[]{:S(2)}, u32[]{:S(2)}) async-start(bf16[8,8,128,128]{3,2,1,0:T(8,128)(2,1)} %get-tuple-element.32), calls=%async_computation.2 | async-start | bytes 4194304 | tf_op jit(solution)/shard_map/all_to_all | solution.py:146
  96.4 1.9 %mul.257 = f32[64,64,128]{2,1,0:T(8,128)} broadcast(f32[64,64]{1,0:T(8,128)S(1)} %exp.43), dimensions={0,1} | broadcast | bytes 2113536 | tf_op jit(solution)/shard_map/mul | solution.py:70
  98.3 1.7 mul.258
  100.2 45.1 %all-to-all-done.2 = bf16[8,8,128,128]{3,2,1,0:T(8,128)(2,1)} async-done(((bf16[8,8,128,128]{3,2,1,0:T(8,128)(2,1)}), bf16[8,8,128,128]{3,2,1,0:T(8,128)(2,1)}, u32[]{:S(2)}, u32[]{:S(2)}) %all-to-all-start.2) | async-done | bytes 2097184 | tf_op jit(solution)/shard_map/all_to_all | solution.py:146
  145.3 2.4 %fusion.4 = f32[64,4,16,128]{3,0,2,1:T(8,128)S(1)} fusion(bf16[64,4,128,1]{2,1,0,3:T(4,128)(2,1)S(1)} %bitcast.89, bf16[4,16,128,128]{3,2,1,0:T(8,128)(2,1)} %bitcast.77), kind=kOutput, calls=%fused_computation.13 | convolution fusion | flops 134217728 | bytes 4259840 | tf_op jit(solution)/shard_map/tgn,gkpn->tgkp/dot_general | solution.py:67
  147.8 2.5 %copy.59 = f32[64,4,16,128]{3,2,1,0:T(8,128)} copy(f32[64,4,16,128]{3,0,2,1:T(8,128)S(1)} %fusion.4) | data formatting | bytes 4194304 | tf_op jit(solution)/shard_map/tgn,gkpn->tgkp/transpose | solution.py:67
  150.3 3.0 %multiply_reduce_fusion = (f32[64,4,16]{0,2,1:T(8,128)S(1)}, f32[64,4,16,128]{3,0,2,1:T(8,128)}) fusion(f32[64,4,16,128]{3,0,2,1:T(8,128)S(1)} %fusion.4, f32[64,4,16]{0,2,1:T(8,128)S(1)} %get-tuple-element.53, bf16[64,4,16,128]{3,2,1,0:T(8,128)(2,1)S(1)} %bitcast.85, f32[4,16,64]{2,1,0:T(8,128)S(1)} %bitcast.98, f32[4,16,64]{2,1,0:T(8,128)S(1)} %bitcast.99, ...), kind=kOutput, calls=%fused_computation.8 | convolution fusion | flops 70512640 | bytes 5378048 | tf_op jit(solution)/shard_map/gkts,sgkp->tgkp/dot_general | solution.py:47
  153.4 2.0 %mul.270 = f32[64,64,128]{2,1,0:T(8,128)} broadcast(f32[64,64]{1,0:T(8,128)S(1)} %copy.60), dimensions={0,1} | broadcast | bytes 2113536 | tf_op jit(solution)/shard_map/mul | solution.py:72
  155.4 2.7 %mul.271 = f32[1,64,8192]{2,1,0:T(8,128)} reshape(f32[64,64,128]{2,1,0:T(8,128)} %mul.270) | data formatting | bytes 4194304 | tf_op jit(solution)/shard_map/mul | solution.py:72
  158.1 4.2 %copy.52 = f32[64,4,16,128]{3,2,1,0:T(8,128)} copy(f32[64,4,16,128]{3,0,2,1:T(8,128)} %get-tuple-element.60) | data formatting | bytes 4194304 | tf_op jit(solution)/shard_map/gkts,sgkp->tgkp/transpose | solution.py:47
  162.3 2.8 %reshape.233 = f32[1,64,8192]{2,1,0:T(8,128)} reshape(f32[64,4,16,128]{3,2,1,0:T(8,128)} %copy.52) | data formatting | bytes 4194304 | tf_op jit(solution)/shard_map/reshape | solution.py:59
  165.0 2.8 %reshape.234 = f32[1,64,8192]{2,1,0:T(8,128)} reshape(f32[64,4,16,128]{3,2,1,0:T(8,128)} %copy.59) | data formatting | bytes 4194304 | tf_op jit(solution)/shard_map/reshape | solution.py:69
  167.8 4.3 %select_convert_fusion = bf16[1,64,8192]{2,1,0:T(8,128)(2,1)} fusion(f32[1,64,8192]{2,1,0:T(8,128)} %mul.271, f32[1,64,8192]{2,1,0:T(8,128)} %reshape.233, f32[1,64,8192]{2,1,0:T(8,128)S(1)} %mul.258, f32[1,64,8192]{2,1,0:T(8,128)} %reshape.234, f32[8192]{0:T(1024)S(1)} %copy-done.4, pred[64]{0:T(512)(128)(4,1)S(1)} %add_compare_fusion), kind=kLoop, calls=%fused_computation.7 | loop fusion | flops 3145728 | bytes 9470016 | tf_op jit(solution)/shard_map/convert_element_type | solution.py:74
  (54 shorter events, 1.7 us)
Async XLA Ops:
  6.5 17.4 %copy-start.2 = (bf16[1,64,8192]{2,1,0:T(8,128)(2,1)S(1)}, bf16[1,64,8192]{2,1,0:T(8,128)(2,1)}, u32[]{:S(2)}) copy-start(bf16[1,64,8192]{2,1,0:T(8,128)(2,1)} %param.13) | copy-start | bytes 3145732
  6.5 17.1 %copy-start.3 = (bf16[1,64,1024]{2,1,0:T(8,128)(2,1)S(1)}, bf16[1,64,1024]{2,1,0:T(8,128)(2,1)}, u32[]{:S(2)}) copy-start(bf16[1,64,1024]{2,1,0:T(8,128)(2,1)} %param.14) | copy-start | bytes 393220
  6.5 17.0 %copy-start.5 = (f32[4,1024]{1,0:T(4,128)S(1)}, f32[4,1024]{1,0:T(4,128)}, u32[]{:S(2)}) copy-start(f32[4,1024]{1,0:T(4,128)} %param.18) | copy-start | bytes 49156
  6.5 58.1 %all-gather.2.cloned.1.call-start = ((), (), s32[]{:S(2)}) async-start(), calls=%async_computation.3 | async-start | bytes 5242880 | tf_op jit(solution)/shard_map/all_gather | solution.py:121
  9.0 14.6 %collective-permute-start = (bf16[3,9216]{1,0:T(4,128)(2,1)S(1)}, bf16[3,9216]{1,0:T(4,128)(2,1)S(1)}, u32[]{:S(2)}, u32[]{:S(2)}) collective-permute-start(bf16[3,9216]{1,0:T(4,128)(2,1)S(1)} %pad_maximum_fusion.2), channel_id=1, source_target_pairs={{0,1},{1,2},{2,3},{3,4},{4,5},{5,6},{6,7},{8,9},{9,10},{10,11},{11... | collective-permute-start | bytes 165896 | tf_op jit(solution)/shard_map/ppermute | solution.py:17
  15.8 14.4 %all-to-all-start = ((bf16[8,1,8]{2,1,0:T(2,128)(2,1)}), bf16[8,1,8]{2,1,0:T(2,128)(2,1)S(1)}, u32[]{:S(2)}, u32[]{:S(2)}) async-start(bf16[8,1,8]{2,1,0:T(2,128)(2,1)} %convert_element_type.119), calls=%async_computation | async-start | bytes 8192 | tf_op jit(solution)/shard_map/all_to_all | solution.py:128
  25.8 1.0 copy-start
  30.2 5.2 %copy-start.6 = (s32[4]{0:T(128)S(1)}, s32[4]{0:T(128)}, u32[]{:S(2)}) copy-start(s32[4]{0:T(128)} %param.22) | copy-start | bytes 52
  30.2 7.1 %copy-start.7 = (s32[4]{0:T(128)S(1)}, s32[4]{0:T(128)}, u32[]{:S(2)}) copy-start(s32[4]{0:T(128)} %param.21) | copy-start | bytes 52
  30.2 54.3 %all-to-all-start.1 = ((bf16[8,8,128,128]{3,2,1,0:T(8,128)(2,1)}), bf16[8,8,128,128]{3,2,1,0:T(8,128)(2,1)S(1)}, u32[]{:S(2)}, u32[]{:S(2)}) async-start(bf16[8,8,128,128]{3,2,1,0:T(8,128)(2,1)} %bitcast.28), calls=%async_computation.1 | async-start | bytes 4194304 | tf_op jit(solution)/shard_map/all_to_all | solution.py:135
  91.9 53.4 %all-to-all-start.2 = ((bf16[8,8,128,128]{3,2,1,0:T(8,128)(2,1)}), bf16[8,8,128,128]{3,2,1,0:T(8,128)(2,1)}, u32[]{:S(2)}, u32[]{:S(2)}) async-start(bf16[8,8,128,128]{3,2,1,0:T(8,128)(2,1)} %get-tuple-element.32), calls=%async_computation.2 | async-start | bytes 4194304 | tf_op jit(solution)/shard_map/all_to_all | solution.py:146
  147.8 2.6 %copy-start.1 = (bf16[8,8,64,128]{3,2,1,0:T(8,128)(2,1)S(1)}, bf16[8,8,64,128]{3,2,1,0:T(8,128)(2,1)}, u32[]{:S(2)}) copy-start(bf16[8,8,64,128]{3,2,1,0:T(8,128)(2,1)} %copy-done) | copy-start | bytes 3145732
  165.0 2.8 %copy-start.4 = (f32[8192]{0:T(1024)S(1)}, f32[8192]{0:T(1024)}, u32[]{:S(2)}) copy-start(f32[8192]{0:T(1024)} %param.19) | copy-start | bytes 98308
Sparse Core Ops, SparseCore 0:
  9.2 55.3 all-gather.1
where the time goes:
time: 180 us; the launch traced here: 179 us
  waiting for transfers between devices  90.8 us (50%)
  local copies, waits for them, and re-layouts  36 us (20%)
  starting transfers between devices  18.1 us (10%)
  between operations  16.2 us (9%)
  matrix products  9.01 us (5%)
  other arithmetic  8.74 us (5%)
    all_to_all x1, waiting for transfers between devices, body(): lax.all_to_all(incoming_parts.astype(jnp.bfloat16), 'ctx', split_axis=0,...  45.1 us
    all_gather x1, waiting for transfers between devices, body(): pooled = lax.all_gather(cache_pool, 'batch', axis=0, tiled=True)  26.1 us
    all_to_all x1, waiting for transfers between devices, body(): lax.all_to_all(end_state.reshape(ctx_count, head_share, P_SIZE, N), 'ctx'...  18.9 us
    all_to_all x1, starting transfers between devices, body(): lax.all_to_all(block_decay.reshape(ctx_count, head_share), 'ctx', split_a...  6.16 us
    dynamic_update_slice x8, local copies, waits for them, and re-layouts, body(): lax.scan(advance, start_state.astype(jnp.float32), (decays_in, states_in))  5.97 us
    all_to_all x1, starting transfers between devices, body(): lax.all_to_all(end_state.reshape(ctx_count, head_share, P_SIZE, N), 'ctx'...  5.24 us
    mul x2, local copies, waits for them, and re-layouts, block_output(): result = summed * inv_scale * norm_gain.reshape(LOCAL_HEADS, P_SIZE)  4.69 us
    all_to_all x1, starting transfers between devices, body(): lax.all_to_all(incoming_parts.astype(jnp.bfloat16), 'ctx', split_axis=0,...  4.35 us
  transfers between devices with their start and end apart: 5, of which 3 were waited for; matrix products, arithmetic and copies ran while one was open for 10% of the time, Pallas kernels for 0%

commit v1 on v0

--- a/solution.py
+++ b/solution.py
@@ -118,7 +118,36 @@
     cache_owner = reuse_owner[request]
     cached_level = reuse_level[request]
     slots = cache_pool.shape[0]
-    pooled = lax.all_gather(cache_pool, "batch", axis=0, tiled=True)
+    current_block, all_values, p_next = (
+        lax.axis_size("batch"),
+        lax.axis_index("batch"),
+        cache_pool.shape[0],
+    )
+    pile = tuple(
+        (to_i * current_block if dev == 0 else to_i for dev, to_i in enumerate(cache_pool.shape))
+    )
+    pooled = lax.dynamic_update_slice_in_dim(
+        jnp.zeros(pile, cache_pool.dtype), cache_pool, all_values * p_next, axis=0
+    )
+    opened = oldest = cache_pool
+    for q in range(1, current_block // 2 + 1):
+        opened = lax.ppermute(
+            opened,
+            axis_name="batch",
+            perm=tuple(((dev, (dev + 1) % current_block) for dev in range(current_block))),
+        )
+        pooled = lax.dynamic_update_slice_in_dim(
+            pooled, opened, (all_values - q) % current_block * p_next, axis=0
+        )
+        if 2 * q < current_block:
+            oldest = lax.ppermute(
+                oldest,
+                axis_name="batch",
+                perm=tuple(((dev, (dev - 1) % current_block) for dev in range(current_block))),
+            )
+            pooled = lax.dynamic_update_slice_in_dim(
+                pooled, oldest, (all_values + q) % current_block * p_next, axis=0
+            )
     slot_index = cache_owner * slots + jnp.maximum(cached_level - 1, 0)
     start_state = lax.dynamic_index_in_dim(pooled, slot_index, 0, keepdims=False)
     start_state = jnp.where(cached_level > 0, start_state, jnp.zeros_like(start_state))

time: 180 us -> 193 us (1.072)
  waiting for transfers between devices: 90.8 us -> 106 us
  between operations: 16.2 us -> 2.69 us
  local copies, waits for them, and re-layouts: 36 us -> 42.5 us
  starting transfers between devices: 18.1 us -> 22 us
    ppermute x0 -> x3, waiting for transfers between devices: none -> 61.1 us  [the longest x2 44.9 us: body(): lax.ppermute(opened, axis_name='batch', perm=tuple(((dev, (dev + 1) % cur...]
    all_gather x1 -> x0, waiting for transfers between devices: 26.1 us -> none  [body(): pooled = lax.all_gather(cache_pool, 'batch', axis=0, tiled=True)]
    all_to_all x1, waiting for transfers between devices: 18.9 us -> 0.01 us  [body(): lax.all_to_all(end_state.reshape(ctx_count, head_share, P_SIZE, N), 'ctx'...]
    dynamic_update_slice x0 -> x4, local copies, waits for them, and re-layouts: none -> 4.34 us  [the longest x2 2.81 us: body(): lax.dynamic_update_slice_in_dim(pooled, opened, (all_values - q) % curren...]
    ppermute x0 -> x3, starting transfers between devices: none -> 3.52 us  [the longest x2 2.08 us: body(): lax.ppermute(opened, axis_name='batch', perm=tuple(((dev, (dev + 1) % cur...]
  transfers between devices with their start and end apart: 5 -> 7, of which waited for: 3 -> 4; matrix products, arithmetic and copies ran while one was open for 10% -> 12% of each run, Pallas kernels for 0% -> 0%
where the time goes in v1:
time: 193 us; the launch traced here: 192 us
  waiting for transfers between devices  106 us (55%)
  local copies, waits for them, and re-layouts  42.5 us (22%)
  starting transfers between devices  22 us (11%)
  matrix products  8.99 us (5%)
  other arithmetic  8.95 us (5%)
  between operations  2.69 us (1%)
    all_to_all x1, waiting for transfers between devices, body(): lax.all_to_all(incoming_parts.astype(jnp.bfloat16), 'ctx', split_axis=0,...  45.2 us
    ppermute x2, waiting for transfers between devices, body(): lax.ppermute(opened, axis_name='batch', perm=tuple(((dev, (dev + 1) % cur...  44.9 us
    ppermute x1, waiting for transfers between devices, body(): lax.ppermute(oldest, axis_name='batch', perm=tuple(((dev, (dev - 1) % cur...  16.2 us
    all_to_all x1, starting transfers between devices, body(): lax.all_to_all(block_decay.reshape(ctx_count, head_share), 'ctx', split_a...  6.16 us
    dynamic_update_slice x8, local copies, waits for them, and re-layouts, body(): lax.scan(advance, start_state.astype(jnp.float32), (decays_in, states_in))  5.97 us
    all_to_all x1, starting transfers between devices, body(): lax.all_to_all(end_state.reshape(ctx_count, head_share, P_SIZE, N), 'ctx'...  5.24 us
    all_to_all x1, starting transfers between devices, body(): lax.all_to_all(incoming_parts.astype(jnp.bfloat16), 'ctx', split_axis=0,...  4.75 us
    mul x2, local copies, waits for them, and re-layouts, block_output(): result = summed * inv_scale * norm_gain.reshape(LOCAL_HEADS, P_SIZE)  4.68 us
  transfers between devices with their start and end apart: 7, of which 4 were waited for; matrix products, arithmetic and copies ran while one was open for 12% of the time, Pallas kernels for 0%

profile of v1, /device:TPU:0, one launch (start us, length us, event | category | flops | bytes accessed | tf_op | source)
XLA Modules:
  0.0 191.6 jit_solution(3679133486284647897)
XLA Ops:
  0.0 1.0 slice_bitcast_fusion
  1.0 0.7 slice_bitcast_fusion.1
  1.8 2.4 %collective-permute-start = (bf16[3,9216]{1,0:T(4,128)(2,1)S(1)}, bf16[3,9216]{1,0:T(4,128)(2,1)S(1)}, u32[]{:S(2)}, u32[]{:S(2)}) collective-permute-start(bf16[3,9216]{1,0:T(4,128)(2,1)S(1)} %pad_maximum_fusion.2), channel_id=1, source_target_pairs={{0,1},{1,2},{2,3},{3,4},{4,5},{5,6},{6,7},{8,9},{9,10},{10,11},{11... | collective-permute-start | bytes 165896 | tf_op jit(solution)/shard_map/ppermute | solution.py:17
  4.2 0.8 copy.48
  5.0 0.7 log.3
  5.7 1.2 dynamic_slice.21
  7.9 0.7 convert_element_type.119
  8.6 6.2 %all-to-all-start = ((bf16[8,1,8]{2,1,0:T(2,128)(2,1)}), bf16[8,1,8]{2,1,0:T(2,128)(2,1)S(1)}, u32[]{:S(2)}, u32[]{:S(2)}) async-start(bf16[8,1,8]{2,1,0:T(2,128)(2,1)} %convert_element_type.119), calls=%async_computation | async-start | bytes 8192 | tf_op jit(solution)/shard_map/all_to_all | solution.py:157
  15.0 1.4 fusion.32
  16.5 0.9 fusion.34
  17.4 1.3 multiply_convert_fusion.5
  18.8 1.6 fusion.16
  20.7 1.0 copy-done
  21.7 3.4 %convolution_convert_fusion = bf16[4,16,128,128]{3,2,1,0:T(8,128)(2,1)} fusion(f32[64,4,16]{0,2,1:T(8,128)S(1)} %get-tuple-element.54, bf16[64,4,16,128]{3,2,1,0:T(8,128)(2,1)S(1)} %bitcast.84, bf16[64,4,128,1]{2,1,0,3:T(4,128)(2,1)S(1)} %bitcast.90), kind=kOutput, calls=%fused_computation.12 | convolution fusion | flops 136839168 | bytes 3227648 | tf_op jit(solution)/shard_map/sgkp,sgn->gkpn/dot_general | solution.py:54
  25.1 5.2 %all-to-all-start.1 = ((bf16[8,8,128,128]{3,2,1,0:T(8,128)(2,1)}), bf16[8,8,128,128]{3,2,1,0:T(8,128)(2,1)S(1)}, u32[]{:S(2)}, u32[]{:S(2)}) async-start(bf16[8,8,128,128]{3,2,1,0:T(8,128)(2,1)} %bitcast.28), calls=%async_computation.1 | async-start | bytes 4194304 | tf_op jit(solution)/shard_map/all_to_all | solution.py:164
  30.4 1.5 collective-permute-start.1
  31.8 1.4 collective-permute-start.2
  33.3 24.2 %collective-permute-done.1 = bf16[4,8,128,128]{3,2,1,0:T(8,128)(2,1)} collective-permute-done((bf16[4,8,128,128]{3,2,1,0:T(8,128)(2,1)}, bf16[4,8,128,128]{3,2,1,0:T(8,128)(2,1)}, u32[]{:S(2)}, u32[]{:S(2)}) %collective-permute-start.1) | collective-permute-done | bytes 1048608 | tf_op jit(solution)/shard_map/ppermute | solution.py:134
  57.5 0.6 collective-permute-start.3
  58.7 0.6 dynamic_slice.23
  61.1 1.0 broadcast_in_dim.63
  62.4 1.4 constant_dynamic-update-slice_fusion.2
  63.9 16.2 %collective-permute-done.2 = bf16[4,8,128,128]{3,2,1,0:T(8,128)(2,1)} collective-permute-done((bf16[4,8,128,128]{3,2,1,0:T(8,128)(2,1)}, bf16[4,8,128,128]{3,2,1,0:T(8,128)(2,1)}, u32[]{:S(2)}, u32[]{:S(2)}) %collective-permute-start.2) | collective-permute-done | bytes 1048608 | tf_op jit(solution)/shard_map/ppermute | solution.py:143
  80.1 1.4 constant_dynamic-update-slice_fusion.1
  81.5 20.6 %collective-permute-done.3 = bf16[4,8,128,128]{3,2,1,0:T(8,128)(2,1)} collective-permute-done((bf16[4,8,128,128]{3,2,1,0:T(8,128)(2,1)}, bf16[4,8,128,128]{3,2,1,0:T(8,128)(2,1)}, u32[]{:S(2)}, u32[]{:S(2)}) %collective-permute-start.3) | collective-permute-done | bytes 1048608 | tf_op jit(solution)/shard_map/ppermute | solution.py:134
  102.1 1.4 constant_dynamic-update-slice_fusion
  103.6 7.4 %while.12 = (s32[]{:T(128)}, f32[8,128,128]{2,1,0:T(8,128)S(1)}, bf16[8,8,128,128]{3,2,1,0:T(8,128)(2,1)}, bf16[8,8]{1,0:T(8,128)(2,1)S(1)}, bf16[8,8,128,128]{3,2,1,0:T(8,128)(2,1)S(1)}, /*index=5*/s32[]{:T(128)}) while((s32[]{:T(128)}, f32[8,128,128]{2,1,0:T(8,128)S(1)}, bf16[8,8,128,128]{3,2,1,0:T(8,128)(2,1)}, bf16[8,8]{1,0:T(8,128)(2,1)S(1)}, ...), condition=%wide.region_2.3_spmd, body=%wide.region_1.2_spmd.sunk | while | flops 393226 | bytes 2359965 | solution.py:172
  103.6 0.7 bitcast_dynamic-update-slice_fusion.2
  104.5 0.7 bitcast_dynamic-update-slice_fusion.2
  105.4 0.7 bitcast_dynamic-update-slice_fusion.2
  106.3 0.8 bitcast_dynamic-update-slice_fusion.2
  107.3 0.7 bitcast_dynamic-update-slice_fusion.2
  108.2 0.7 bitcast_dynamic-update-slice_fusion.2
  109.1 0.8 bitcast_dynamic-update-slice_fusion.2
  110.1 0.7 bitcast_dynamic-update-slice_fusion.2
  111.0 4.8 %all-to-all-start.2 = ((bf16[8,8,128,128]{3,2,1,0:T(8,128)(2,1)}), bf16[8,8,128,128]{3,2,1,0:T(8,128)(2,1)}, u32[]{:S(2)}, u32[]{:S(2)}) async-start(bf16[8,8,128,128]{3,2,1,0:T(8,128)(2,1)} %get-tuple-element.32), calls=%async_computation.2 | async-start | bytes 4194304 | tf_op jit(solution)/shard_map/all_to_all | solution.py:175
  115.8 1.9 %mul.269 = f32[64,64,128]{2,1,0:T(8,128)} broadcast(f32[64,64]{1,0:T(8,128)S(1)} %exp.43), dimensions={0,1} | broadcast | bytes 2113536 | tf_op jit(solution)/shard_map/mul | solution.py:70
  117.8 1.7 mul.270
  119.7 45.2 %all-to-all-done.2 = bf16[8,8,128,128]{3,2,1,0:T(8,128)(2,1)} async-done(((bf16[8,8,128,128]{3,2,1,0:T(8,128)(2,1)}), bf16[8,8,128,128]{3,2,1,0:T(8,128)(2,1)}, u32[]{:S(2)}, u32[]{:S(2)}) %all-to-all-start.2) | async-done | bytes 2097184 | tf_op jit(solution)/shard_map/all_to_all | solution.py:175
  164.9 2.4 %fusion.4 = f32[64,4,16,128]{3,0,2,1:T(8,128)S(1)} fusion(bf16[64,4,128,1]{2,1,0,3:T(4,128)(2,1)S(1)} %bitcast.89, bf16[4,16,128,128]{3,2,1,0:T(8,128)(2,1)} %bitcast.77), kind=kOutput, calls=%fused_computation.13 | convolution fusion | flops 134217728 | bytes 4259840 | tf_op jit(solution)/shard_map/tgn,gkpn->tgkp/dot_general | solution.py:67
  167.4 2.5 %copy.59 = f32[64,4,16,128]{3,2,1,0:T(8,128)} copy(f32[64,4,16,128]{3,0,2,1:T(8,128)S(1)} %fusion.4) | data formatting | bytes 4194304 | tf_op jit(solution)/shard_map/tgn,gkpn->tgkp/transpose | solution.py:67
  169.9 3.0 %multiply_reduce_fusion = (f32[64,4,16]{0,2,1:T(8,128)S(1)}, f32[64,4,16,128]{3,0,2,1:T(8,128)}) fusion(f32[64,4,16,128]{3,0,2,1:T(8,128)S(1)} %fusion.4, f32[64,4,16]{0,2,1:T(8,128)S(1)} %get-tuple-element.53, bf16[64,4,16,128]{3,2,1,0:T(8,128)(2,1)S(1)} %bitcast.85, f32[4,16,64]{2,1,0:T(8,128)S(1)} %bitcast.98, f32[4,16,64]{2,1,0:T(8,128)S(1)} %bitcast.99, ...), kind=kOutput, calls=%fused_computation.8 | convolution fusion | flops 70512640 | bytes 5378048 | tf_op jit(solution)/shard_map/gkts,sgkp->tgkp/dot_general | solution.py:47
  173.0 2.0 %mul.286 = f32[64,64,128]{2,1,0:T(8,128)} broadcast(f32[64,64]{1,0:T(8,128)S(1)} %copy.60), dimensions={0,1} | broadcast | bytes 2113536 | tf_op jit(solution)/shard_map/mul | solution.py:72
  174.9 2.7 %mul.287 = f32[1,64,8192]{2,1,0:T(8,128)} reshape(f32[64,64,128]{2,1,0:T(8,128)} %mul.286) | data formatting | bytes 4194304 | tf_op jit(solution)/shard_map/mul | solution.py:72
  177.7 4.1 %copy.52 = f32[64,4,16,128]{3,2,1,0:T(8,128)} copy(f32[64,4,16,128]{3,0,2,1:T(8,128)} %get-tuple-element.60) | data formatting | bytes 4194304 | tf_op jit(solution)/shard_map/gkts,sgkp->tgkp/transpose | solution.py:47
  181.8 2.7 %reshape.233 = f32[1,64,8192]{2,1,0:T(8,128)} reshape(f32[64,4,16,128]{3,2,1,0:T(8,128)} %copy.52) | data formatting | bytes 4194304 | tf_op jit(solution)/shard_map/reshape | solution.py:59
  184.6 2.8 %reshape.234 = f32[1,64,8192]{2,1,0:T(8,128)} reshape(f32[64,4,16,128]{3,2,1,0:T(8,128)} %copy.59) | data formatting | bytes 4194304 | tf_op jit(solution)/shard_map/reshape | solution.py:69
  187.3 4.3 %select_convert_fusion = bf16[1,64,8192]{2,1,0:T(8,128)(2,1)} fusion(f32[1,64,8192]{2,1,0:T(8,128)} %mul.287, f32[1,64,8192]{2,1,0:T(8,128)} %reshape.233, f32[1,64,8192]{2,1,0:T(8,128)S(1)} %mul.270, f32[1,64,8192]{2,1,0:T(8,128)} %reshape.234, f32[8192]{0:T(1024)S(1)} %copy-done.4, pred[64]{0:T(512)(128)(4,1)S(1)} %add_compare_fusion), kind=kLoop, calls=%fused_computation.7 | loop fusion | flops 3145728 | bytes 9470016 | tf_op jit(solution)/shard_map/convert_element_type | solution.py:74
  (60 shorter events, 3.6 us)
Async XLA Ops:
  0.0 18.8 %copy-start.2 = (bf16[1,64,8192]{2,1,0:T(8,128)(2,1)S(1)}, bf16[1,64,8192]{2,1,0:T(8,128)(2,1)}, u32[]{:S(2)}) copy-start(bf16[1,64,8192]{2,1,0:T(8,128)(2,1)} %param.13) | copy-start | bytes 3145732
  1.8 15.6 %collective-permute-start = (bf16[3,9216]{1,0:T(4,128)(2,1)S(1)}, bf16[3,9216]{1,0:T(4,128)(2,1)S(1)}, u32[]{:S(2)}, u32[]{:S(2)}) collective-permute-start(bf16[3,9216]{1,0:T(4,128)(2,1)S(1)} %pad_maximum_fusion.2), channel_id=1, source_target_pairs={{0,1},{1,2},{2,3},{3,4},{4,5},{5,6},{6,7},{8,9},{9,10},{10,11},{11... | collective-permute-start | bytes 165896 | tf_op jit(solution)/shard_map/ppermute | solution.py:17
  8.6 16.5 %all-to-all-start = ((bf16[8,1,8]{2,1,0:T(2,128)(2,1)}), bf16[8,1,8]{2,1,0:T(2,128)(2,1)S(1)}, u32[]{:S(2)}, u32[]{:S(2)}) async-start(bf16[8,1,8]{2,1,0:T(2,128)(2,1)} %convert_element_type.119), calls=%async_computation | async-start | bytes 8192 | tf_op jit(solution)/shard_map/all_to_all | solution.py:157
  20.7 1.0 copy-start
  25.1 33.0 %copy-start.5 = (s32[4]{0:T(128)S(1)}, s32[4]{0:T(128)}, u32[]{:S(2)}) copy-start(s32[4]{0:T(128)} %param.22) | copy-start | bytes 52
  25.1 33.6 %copy-start.6 = (s32[4]{0:T(128)S(1)}, s32[4]{0:T(128)}, u32[]{:S(2)}) copy-start(s32[4]{0:T(128)} %param.21) | copy-start | bytes 52
  25.1 78.4 %all-to-all-start.1 = ((bf16[8,8,128,128]{3,2,1,0:T(8,128)(2,1)}), bf16[8,8,128,128]{3,2,1,0:T(8,128)(2,1)S(1)}, u32[]{:S(2)}, u32[]{:S(2)}) async-start(bf16[8,8,128,128]{3,2,1,0:T(8,128)(2,1)} %bitcast.28), calls=%async_computation.1 | async-start | bytes 4194304 | tf_op jit(solution)/shard_map/all_to_all | solution.py:164
  30.4 27.2 %collective-permute-start.1 = (bf16[4,8,128,128]{3,2,1,0:T(8,128)(2,1)}, bf16[4,8,128,128]{3,2,1,0:T(8,128)(2,1)}, u32[]{:S(2)}, u32[]{:S(2)}) collective-permute-start(bf16[4,8,128,128]{3,2,1,0:T(8,128)(2,1)} %param.20), channel_id=1, source_target_pairs={{0,8},{8,16},{16,24},{24,0},{1,9},{9,17},{17,25},{25,1},{2,10},{10... | collective-permute-start | bytes 3145736 | tf_op jit(solution)/shard_map/ppermute | solution.py:134
  31.8 48.2 %collective-permute-start.2 = (bf16[4,8,128,128]{3,2,1,0:T(8,128)(2,1)}, bf16[4,8,128,128]{3,2,1,0:T(8,128)(2,1)}, u32[]{:S(2)}, u32[]{:S(2)}) collective-permute-start(bf16[4,8,128,128]{3,2,1,0:T(8,128)(2,1)} %param.20), channel_id=1, source_target_pairs={{0,24},{8,0},{16,8},{24,16},{1,25},{9,1},{17,9},{25,17},{2,26},{10... | collective-permute-start | bytes 3145736 | tf_op jit(solution)/shard_map/ppermute | solution.py:143
  57.5 44.6 %collective-permute-start.3 = (bf16[4,8,128,128]{3,2,1,0:T(8,128)(2,1)}, bf16[4,8,128,128]{3,2,1,0:T(8,128)(2,1)}, u32[]{:S(2)}, u32[]{:S(2)}) collective-permute-start(bf16[4,8,128,128]{3,2,1,0:T(8,128)(2,1)} %collective-permute-done.1), channel_id=1, source_target_pairs={{0,8},{8,16},{16,24},{24,0},{1,9},{9,17},{17,25},{25,1},{2,10},{10... | collective-permute-start | bytes 3145736 | tf_op jit(solution)/shard_map/ppermute | solution.py:134
  61.1 1.2 copy-start.3
  111.0 53.9 %all-to-all-start.2 = ((bf16[8,8,128,128]{3,2,1,0:T(8,128)(2,1)}), bf16[8,8,128,128]{3,2,1,0:T(8,128)(2,1)}, u32[]{:S(2)}, u32[]{:S(2)}) async-start(bf16[8,8,128,128]{3,2,1,0:T(8,128)(2,1)} %get-tuple-element.32), calls=%async_computation.2 | async-start | bytes 4194304 | tf_op jit(solution)/shard_map/all_to_all | solution.py:175
  167.3 2.6 %copy-start.1 = (bf16[8,8,64,128]{3,2,1,0:T(8,128)(2,1)S(1)}, bf16[8,8,64,128]{3,2,1,0:T(8,128)(2,1)}, u32[]{:S(2)}) copy-start(bf16[8,8,64,128]{3,2,1,0:T(8,128)(2,1)} %copy-done) | copy-start | bytes 3145732
  184.6 2.8 %copy-start.4 = (f32[8192]{0:T(1024)S(1)}, f32[8192]{0:T(1024)}, u32[]{:S(2)}) copy-start(f32[8192]{0:T(1024)} %param.19) | copy-start | bytes 98308
